TPU v7x, 512 devices: a whole 4x8x8 slice. The times are simulated.
512 devices in a mesh: row: 8 (over y), col: 16 (over x_lo, z), layer: 4 (over x_hi, core).
Axes of the slice: x: 4 (x_hi: 2, x_lo: 2; x = x_hi * 2 + x_lo), y: 8, z: 8, core: 2. Of those that a mesh axis runs over, the one named last changes fastest.
Arguments:
- integrals: bfloat16 [64, 1024, 3072], P('layer', 'col', 'row'), may hold values from -0.0234375 to 0.0234375
- amplitudes: bfloat16 [64, 1024, 2048], P('layer', 'row', 'col'), may hold values from -6 to 6
- coulomb: bfloat16 [3072, 2048], P(('row', 'layer'), 'col'), may hold values from -6 to 6
- row_gap: float32 [3072], P(('row', 'layer')), may hold values from 0.5 to 4
- col_gap: float32 [2048], P('col'), may hold values from 0.5 to 4
Outputs:
- residual: float32 [3072, 2048], P(('row', 'layer'), 'col')
All inputs are finite; a program needn't handle non-finite values.
Results may differ from a plain program's by a relative error of at most 0.0003.
Values may be sent and summed in bfloat16 or wider, within the bound.
No kernel may reach another device: no remote copies, remote signals or barrier semaphores. Data moves between devices by JAX's collectives and lax.ppermute only.
A program may use at most 64 MiB of HBM per device.

v0:
```python
import jax
import jax.numpy as jnp
from jax import lax
from jax.sharding import PartitionSpec as P


def local(integrals, amplitudes, coulomb, row_gap, col_gap):
    contract = (((0, 1), (0, 1)), ((), ()))
    gathered = lax.all_gather(amplitudes, "row", axis=1, tiled=True)
    partial_sum = lax.dot_general(
        lax.all_gather(integrals, "col", axis=1, tiled=True),
        gathered,
        contract,
        preferred_element_type=jnp.float32,
    )
    share_rows = coulomb.shape[0]
    summed_all = lax.psum(partial_sum, "layer")
    own_rows = lax.dynamic_slice_in_dim(
        summed_all, lax.axis_index("layer") * share_rows, share_rows, 0
    )
    gap_sum = row_gap[:, None] + col_gap[None, :]
    return (coulomb.astype(jnp.float32) + own_rows) / gap_sum


def solution(mesh):
    placed = (
        P("layer", "col", "row"),
        P("layer", "row", "col"),
        P(("row", "layer"), "col"),
        P(("row", "layer")),
        P("col"),
    )
    return jax.shard_map(
        local, mesh=mesh, in_specs=placed, out_specs=P(("row", "layer"), "col"), check_vma=False
    )
```

profile of v0, /device:TPU:1, one launch (start us, length us, event | category | flops | bytes accessed | tf_op | source)
XLA Modules:
  0.0 286.8 jit_solution(3546155924513565021)
XLA Ops:
  6.5 0.0 copy-start
  6.5 0.0 copy-start.1
  6.5 0.0 copy-start.2
  6.5 0.0 all-gather.5.cloned.1.call-start
  6.5 0.7 all-gather.5.cloned.1.call-update
  7.3 0.0 all-gather.3.cloned.1.call-start
  7.3 0.7 all-gather.3.cloned.1.call-update
  8.0 0.0 all-reduce.2.cloned.1.call-start
  8.1 64.0 %all-gather.5.cloned.1.call-done = bf16[16,1024,128]{2,1,0:T(8,128)(2,1)} async-done(((bf16[16,128,128]{2,1,0:T(8,128)(2,1)}), bf16[16,1024,128]{2,1,0:T(8,128)(2,1)}) %all-gather.5.cloned.1.call-update) | async-done | bytes 4194320 | tf_op jit(solution)/shard_map/all_gather | solution.py:9
  72.1 147.7 %all-gather.3.cloned.1.call-done = bf16[16,1024,384]{2,1,0:T(8,128)(2,1)} async-done(((bf16[16,64,384]{2,1,0:T(8,128)(2,1)}), bf16[16,1024,384]{2,1,0:T(8,128)(2,1)}) %all-gather.3.cloned.1.call-update) | async-done | bytes 12582928 | tf_op jit(solution)/shard_map/all_gather | solution.py:11
  219.8 9.9 %convolution_bitcast_fusion = f32[384,128]{1,0:T(8,128)} fusion(bf16[16,1024,384]{2,1,0:T(8,128)(2,1)} %all-gather.3.cloned.1.call-done, bf16[16,1024,128]{2,1,0:T(8,128)(2,1)} %all-gather.5.cloned.1.call-done), kind=kOutput, calls=%fused_computation | convolution fusion | flops 1610612736 | bytes 16973824 | tf_op jit(solution)/shard_map/dot_general | solution.py:10
  229.7 0.0 all-reduce.2.cloned.1.call-update
  229.7 49.0 %all-reduce.2.cloned.1.call-done = f32[384,128]{1,0:T(8,128)} async-done(((f32[384,128]{1,0:T(8,128)}), f32[384,128]{1,0:T(8,128)}) %all-reduce.2.cloned.1.call-update) | async-done | bytes 196624 | tf_op jit(solution)/shard_map/psum | solution.py:17
  278.7 0.0 copy-done
  278.7 0.0 copy-done.1
  278.7 0.0 copy-done.2
  278.7 1.5 add_divide_fusion
Async XLA Ops:
  6.5 272.2 %copy-start = (bf16[96,128]{1,0:T(8,128)(2,1)S(1)}, bf16[96,128]{1,0:T(8,128)(2,1)}, u32[]{:S(2)}) copy-start(bf16[96,128]{1,0:T(8,128)(2,1)} %param.7) | copy-start | bytes 73732
  6.5 272.2 %copy-start.1 = (f32[128]{0:T(128)S(1)}, f32[128]{0:T(128)}, u32[]{:S(2)}) copy-start(f32[128]{0:T(128)} %param.9) | copy-start | bytes 1540
  6.5 272.2 %copy-start.2 = (f32[96]{0:T(128)S(1)}, f32[96]{0:T(128)}, u32[]{:S(2)}) copy-start(f32[96]{0:T(128)} %param.8) | copy-start | bytes 1156
  6.5 65.6 %all-gather.5.cloned.1.call-start = ((), (), s32[]{:S(2)}) async-start(), calls=%async_computation.1 | async-start | bytes 4718592 | tf_op jit(solution)/shard_map/all_gather | solution.py:9
  7.3 212.5 %all-gather.3.cloned.1.call-start = ((), (), s32[]{:S(2)}) async-start(), calls=%async_computation | async-start | bytes 13369344 | tf_op jit(solution)/shard_map/all_gather | solution.py:11
  8.0 270.7 %all-reduce.2.cloned.1.call-start = ((), (), s32[]{:S(2)}) async-start(), calls=%async_computation.2 | async-start | bytes 393216 | tf_op jit(solution)/shard_map/psum | solution.py:17
Sparse Core Ops, SparseCore 0:
  9.4 62.6 all-gather.4
  74.2 145.5 all-gather.2
  229.8 48.8 all-reduce.1
where the time goes:
time: 287 us
  waiting for transfers between devices  262 us (91%)
  between operations  13.1 us (5%)
  matrix products  9.89 us (3%)
    all_gather x1, waiting for transfers between devices, local(): lax.all_gather(integrals, 'col', axis=1, tiled=True)  148 us
    all_gather x1, waiting for transfers between devices, local(): gathered = lax.all_gather(amplitudes, 'row', axis=1, tiled=True)  64 us
    psum x1, waiting for transfers between devices, local(): summed_all = lax.psum(partial_sum, 'layer')  49 us
    dot_general x1, matrix products, local(): lax.dot_general(lax.all_gather(integrals, 'col', axis=1, tiled=True), gat...  9.89 us
  transfers between devices with their start and end apart: 3, of which 3 were waited for; matrix products, arithmetic and copies ran while one was open for 0% of the time, Pallas kernels for 0%

commit v1 on v0

--- a/solution.py
+++ b/solution.py
@@ -4,14 +4,18 @@
 from jax.sharding import PartitionSpec as P
 
 
+def all_by_exchange(x, mesh_axis, dim):
+    size = lax.axis_size(mesh_axis)
+    parts = jnp.stack([x for _ in range(size)])
+    parts = lax.all_to_all(parts, mesh_axis, split_axis=0, concat_axis=0)
+    return jnp.concatenate(parts, axis=dim)
+
+
 def local(integrals, amplitudes, coulomb, row_gap, col_gap):
     contract = (((0, 1), (0, 1)), ((), ()))
     gathered = lax.all_gather(amplitudes, "row", axis=1, tiled=True)
     partial_sum = lax.dot_general(
-        lax.all_gather(integrals, "col", axis=1, tiled=True),
-        gathered,
-        contract,
-        preferred_element_type=jnp.float32,
+        all_by_exchange(integrals, "col", 1), gathered, contract, preferred_element_type=jnp.float32
     )
     share_rows = coulomb.shape[0]
     summed_all = lax.psum(partial_sum, "layer")

time: 287 us -> 396 us (1.38)
  waiting for transfers between devices: 262 us -> 340 us
  local copies, waits for them, and re-layouts: 0.01 us -> 18.5 us
  starting transfers between devices: 0.08 us -> 12 us
    all_to_all x0 -> x1, waiting for transfers between devices: none -> 278 us  [all_by_exchange(): parts = lax.all_to_all(parts, mesh_axis, split_axis=0, concat_axis=0)]
    all_gather x1 -> x0, waiting for transfers between devices: 148 us -> none  [local(): lax.all_gather(integrals, 'col', axis=1, tiled=True)]
    all_gather x1, waiting for transfers between devices: 64 us -> 0.02 us  [local(): gathered = lax.all_gather(amplitudes, 'row', axis=1, tiled=True)]
    psum x1, waiting for transfers between devices: 49 us -> 61.4 us  [local(): summed_all = lax.psum(partial_sum, 'layer')]
    all_to_all x0 -> x1, starting transfers between devices: none -> 11.9 us  [all_by_exchange(): parts = lax.all_to_all(parts, mesh_axis, split_axis=0, concat_axis=0)]
    all_to_all x0 -> x1, local copies, waits for them, and re-layouts: none -> 10.8 us  [all_by_exchange(): parts = lax.all_to_all(parts, mesh_axis, split_axis=0, concat_axis=0)]
    another operation x0 -> x1, local copies, waits for them, and re-layouts: none -> 7.74 us  [all_by_exchange(): parts = jnp.stack([x for _ in range(size)])]
  transfers between devices with their start and end apart: 3 -> 3, of which waited for: 3 -> 2; matrix products, arithmetic and copies ran while one was open for 0% -> 3% of each run, Pallas kernels for 0% -> 0%
where the time goes in v1:
time: 396 us
  waiting for transfers between devices  340 us (86%)
  local copies, waits for them, and re-layouts  18.5 us (5%)
  between operations  13.4 us (3%)
  starting transfers between devices  12 us (3%)
  matrix products  9.89 us (2%)
    all_to_all x1, waiting for transfers between devices, all_by_exchange(): parts = lax.all_to_all(parts, mesh_axis, split_axis=0, concat_axis=0)  278 us
    psum x1, waiting for transfers between devices, local(): summed_all = lax.psum(partial_sum, 'layer')  61.4 us
    all_to_all x1, starting transfers between devices, all_by_exchange(): parts = lax.all_to_all(parts, mesh_axis, split_axis=0, concat_axis=0)  11.9 us
    all_to_all x1, local copies, waits for them, and re-layouts, all_by_exchange(): parts = lax.all_to_all(parts, mesh_axis, split_axis=0, concat_axis=0)  10.8 us
    dot_general x1, matrix products, local(): lax.dot_general(all_by_exchange(integrals, 'col', 1), gathered, contract,...  9.89 us
  transfers between devices with their start and end apart: 3, of which 2 were waited for; matrix products, arithmetic and copies ran while one was open for 3% of the time, Pallas kernels for 0%

profile of v1, /device:TPU:1, one launch (start us, length us, event | category | flops | bytes accessed | tf_op | source)
XLA Modules:
  0.0 395.8 jit_solution(7481548405916938383)
XLA Ops:
  6.5 7.7 %stack.2 = bf16[16,16,64,384]{3,2,1,0:T(8,128)(2,1)} broadcast(bf16[16,64,384]{2,1,0:T(8,128)(2,1)} %param.5), dimensions={1,2,3} | broadcast | bytes 13369344 | tf_op jit(solution)/shard_map/stack | solution.py:9
  14.3 11.9 %all-to-all-start = ((bf16[16,16,64,384]{3,2,1,0:T(8,128)(2,1)}), bf16[16,16,64,384]{3,2,1,0:T(8,128)(2,1)}, u32[]{:S(2)}, u32[]{:S(2)}) async-start(bf16[16,16,64,384]{3,2,1,0:T(8,128)(2,1)} %stack.2), calls=%async_computation | async-start | bytes 25165824 | tf_op jit(solution)/shard_map/all_to_all | solution.py:10
  26.2 0.0 all-gather.2.cloned.1.call-start
  26.3 0.7 all-gather.2.cloned.1.call-update
  27.0 0.0 all-reduce.2.cloned.1.call-start
  27.0 278.3 %all-to-all-done = bf16[16,16,64,384]{3,2,1,0:T(8,128)(2,1)} async-done(((bf16[16,16,64,384]{3,2,1,0:T(8,128)(2,1)}), bf16[16,16,64,384]{3,2,1,0:T(8,128)(2,1)}, u32[]{:S(2)}, u32[]{:S(2)}) %all-to-all-start) | async-done | bytes 12582944 | tf_op jit(solution)/shard_map/all_to_all | solution.py:10
  305.3 10.8 %copy.8 = bf16[16,16,64,384]{3,2,0,1:T(8,128)(2,1)} copy(bf16[16,16,64,384]{3,2,1,0:T(8,128)(2,1)} %all-to-all-done) | data formatting | bytes 25165824 | tf_op jit(solution)/shard_map/all_to_all | solution.py:10
  316.1 0.0 copy-start
  316.1 0.0 copy-start.1
  316.1 0.0 copy-start.2
  316.1 0.0 all-gather.2.cloned.1.call-done
  316.1 9.9 %convolution_bitcast_fusion = f32[384,128]{1,0:T(8,128)} fusion(bf16[16,1024,384]{2,1,0:T(8,128)(2,1)} %bitcast.7, bf16[16,1024,128]{2,1,0:T(8,128)(2,1)} %all-gather.2.cloned.1.call-done), kind=kOutput, calls=%fused_computation | convolution fusion | flops 1610612736 | bytes 16973824 | tf_op jit(solution)/shard_map/dot_general | solution.py:17
  326.0 0.0 all-reduce.2.cloned.1.call-update
  326.0 61.4 %all-reduce.2.cloned.1.call-done = f32[384,128]{1,0:T(8,128)} async-done(((f32[384,128]{1,0:T(8,128)}), f32[384,128]{1,0:T(8,128)}) %all-reduce.2.cloned.1.call-update) | async-done | bytes 196624 | tf_op jit(solution)/shard_map/psum | solution.py:21
  387.4 0.0 copy-done
  387.5 0.0 copy-done.1
  387.5 0.0 copy-done.2
  387.5 1.5 add_divide_fusion
Async XLA Ops:
  14.3 291.0 %all-to-all-start = ((bf16[16,16,64,384]{3,2,1,0:T(8,128)(2,1)}), bf16[16,16,64,384]{3,2,1,0:T(8,128)(2,1)}, u32[]{:S(2)}, u32[]{:S(2)}) async-start(bf16[16,16,64,384]{3,2,1,0:T(8,128)(2,1)} %stack.2), calls=%async_computation | async-start | bytes 25165824 | tf_op jit(solution)/shard_map/all_to_all | solution.py:10
  26.2 289.9 %all-gather.2.cloned.1.call-start = ((), (), s32[]{:S(2)}) async-start(), calls=%async_computation.1 | async-start | bytes 4718592 | tf_op jit(solution)/shard_map/all_gather | solution.py:16
  27.0 360.5 %all-reduce.2.cloned.1.call-start = ((), (), s32[]{:S(2)}) async-start(), calls=%async_computation.2 | async-start | bytes 393216 | tf_op jit(solution)/shard_map/psum | solution.py:21
  316.1 71.4 %copy-start = (bf16[96,128]{1,0:T(8,128)(2,1)S(1)}, bf16[96,128]{1,0:T(8,128)(2,1)}, u32[]{:S(2)}) copy-start(bf16[96,128]{1,0:T(8,128)(2,1)} %param.7) | copy-start | bytes 73732
  316.1 71.4 %copy-start.1 = (f32[128]{0:T(128)S(1)}, f32[128]{0:T(128)}, u32[]{:S(2)}) copy-start(f32[128]{0:T(128)} %param.9) | copy-start | bytes 1540
  316.1 71.4 %copy-start.2 = (f32[96]{0:T(128)S(1)}, f32[96]{0:T(128)}, u32[]{:S(2)}) copy-start(f32[96]{0:T(128)} %param.8) | copy-start | bytes 1156
Sparse Core Ops, SparseCore 0:
  29.2 58.5 all-gather.1
  326.2 61.2 all-reduce.1
